TPU v7x, 256 devices: a whole 4x4x8 slice. The times are simulated.
256 devices in a mesh: owner: 64 (over z, y, core), aux: 4 (over x).
Axes of the slice: x: 4, y: 4, z: 8, core: 2. Of those that a mesh axis runs over, the one named last changes fastest.
Arguments:
- blocks: bfloat16 [256, 256, 2048], P('owner', None, 'aux'), may hold values from -0.890625 to 0.890625
- wanted: int32 [64, 64, 1], P('owner'), may hold values from 0 to 3
- pair_local: int32 [64, 64], P('owner'), may hold values from 0 to 3
- pair_slot: int32 [64, 64], P('owner'), may hold values from 0 to 63, each once within a row
- pno_local: bfloat16 [64, 64, 256, 128], P('owner'), may hold values from -0.375 to 0.375
- pno_remote: bfloat16 [64, 64, 256, 128], P('owner'), may hold values from -0.375 to 0.375
Outputs:
- integrals: bfloat16 [64, 64, 128, 128], P('owner', 'aux')
Inputs may be any that keep to these rules, and one draw needn't show every extreme that they name: pair_slot is a permutation of the requests of each owner.
All inputs are finite; a program needn't handle non-finite values.
Results may differ from a plain program's by a relative error of at most 0.0057.
Values may be sent and summed in bfloat16 or wider, within the bound.
A program may use at most 128 MiB of HBM per device.

v0:
```python
import jax
import jax.numpy as jnp
from jax import lax
from jax.sharding import PartitionSpec as P


def project(maps, tiles):
    return jnp.einsum("pdk,pdq->pkq", maps, tiles, preferred_element_type=jnp.float32).astype(
        jnp.bfloat16
    )


def body(blocks, wanted, pair_local, pair_slot, pno_local, pno_remote):
    served = lax.all_to_all(wanted, "owner", split_axis=1, concat_axis=0, tiled=True).reshape(-1)
    chosen = jnp.take(blocks, served, axis=0)
    arrived = lax.all_to_all(chosen, "owner", split_axis=0, concat_axis=0, tiled=True)
    right = project(pno_remote[0], arrived)
    right = jnp.take(right, pair_slot[0], axis=0)
    first_blocks = jnp.take(blocks, pair_local[0], axis=0)
    left = project(pno_local[0], first_blocks)
    summed = lax.psum_scatter(
        jnp.einsum("pkq,plq->pkl", left, right, preferred_element_type=jnp.float32),
        "aux",
        scatter_dimension=0,
        tiled=True,
    )
    return summed.astype(jnp.bfloat16)[None]


def solution(mesh):
    in_specs = (
        P("owner", None, "aux"),
        P("owner", None, None),
        P("owner", None),
        P("owner", None),
        P("owner", None, None, None),
        P("owner", None, None, None),
    )
    out_specs = P("owner", "aux", None, None)
    return jax.shard_map(body, mesh=mesh, in_specs=in_specs, out_specs=out_specs, check_vma=False)
```

profile of v0, /device:TPU:1, one launch (start us, length us, event | category | flops | bytes accessed | tf_op | source)
XLA Modules:
  0.0 556.8 jit_solution(11488651335553884820)
XLA Ops:
  6.5 0.0 copy-start
  6.5 0.8 copy.12
  7.4 22.3 %all_to_all.14 = s32[1,64,1]{2,0,1:T(1,128)S(1)} all-to-all(s32[1,64,1]{2,0,1:T(1,128)S(1)} %copy.12), channel_id=1, replica_groups=mesh['owner'=64,'aux'=4] {'owner'}, dimensions={1} | all-to-all | bytes 512 | tf_op jit(solution)/shard_map/all_to_all | solution.py:14
  29.7 1.2 reduce
  31.0 0.0 copy-done
  31.0 7.5 %gather_fusion.2 = bf16[64,256,512]{2,1,0:T(8,128)(2,1)} fusion(bf16[4,256,512]{2,1,0:T(8,128)(2,1)S(1)} %copy-done, s32[1024]{0:T(1024)S(1)} %pad_clamp_fusion.1), kind=kCustom, calls=%fused_computation.1.clone | custom fusion | bytes 33554688 | tf_op jit(solution)/shard_map/jit(_take)/gather | solution.py:15
  38.5 22.4 %copy.13 = bf16[64,256,512]{1,2,0:T(8,128)(2,1)} copy(bf16[64,256,512]{2,1,0:T(8,128)(2,1)} %gather_fusion.2) | data formatting | bytes 33554432 | tf_op jit(solution)/shard_map/jit(_take)/gather | solution.py:15
  60.9 14.2 %broadcast_select_fusion = bf16[64,256,512]{1,2,0:T(8,128)(2,1)} fusion(bf16[64,256,512]{1,2,0:T(8,128)(2,1)} %copy.13, pred[64]{0:T(512)(128)(4,1)S(1)} %compare_and_fusion), kind=kLoop, calls=%fused_computation.5 | loop fusion | flops 8388608 | bytes 33554496 | tf_op jit(solution)/shard_map/jit(_take)/select_n | solution.py:15
  75.0 0.0 copy-start.3
  75.0 6.0 %all-to-all-start.1 = ((bf16[64,256,512]{1,2,0:T(8,128)(2,1)}), bf16[64,256,512]{1,2,0:T(8,128)(2,1)}, u32[]{:S(2)}, u32[]{:S(2)}) async-start(bf16[64,256,512]{1,2,0:T(8,128)(2,1)} %broadcast_select_fusion), calls=%async_computation.1 | async-start | bytes 33554432 | tf_op jit(solution)/shard_map/all_to_all | solution.py:16
  81.0 0.2 reduce-scatter.2.cloned.1.call-start
  81.2 0.0 copy-done.3
  81.3 0.0 copy-start.2
  81.3 7.5 %gather_fusion.1 = bf16[64,256,512]{2,1,0:T(8,128)(2,1)} fusion(bf16[4,256,512]{2,1,0:T(8,128)(2,1)S(1)} %copy-done, s32[1024]{0:T(1024)S(1)} %pad_clamp_fusion.2), kind=kCustom, calls=%fused_computation.clone | custom fusion | bytes 33554688 | tf_op jit(solution)/shard_map/jit(_take)/gather | solution.py:19
  88.8 0.0 copy-done.2
  88.8 356.8 %all-to-all-done.1 = bf16[64,256,512]{1,2,0:T(8,128)(2,1)} async-done(((bf16[64,256,512]{1,2,0:T(8,128)(2,1)}), bf16[64,256,512]{1,2,0:T(8,128)(2,1)}, u32[]{:S(2)}, u32[]{:S(2)}) %all-to-all-start.1) | async-done | bytes 16777248 | tf_op jit(solution)/shard_map/all_to_all | solution.py:16
  445.6 11.3 %convert_bitcast_fusion = bf16[64,128,512]{1,2,0:T(8,128)(2,1)} fusion(bf16[64,256,512]{1,2,0:T(8,128)(2,1)} %all-to-all-done.1, bf16[1,64,256,128]{3,2,1,0:T(8,128)(2,1)} %param.13), kind=kOutput, calls=%fused_computation.10 | convolution fusion | flops 2151677952 | bytes 29360128 | tf_op jit(solution)/shard_map/pdk,pdq->pkq/dot_general | solution.py:8
  457.0 11.9 %copy.14 = bf16[64,128,512]{2,1,0:T(8,128)(2,1)} copy(bf16[64,128,512]{1,2,0:T(8,128)(2,1)} %convert_bitcast_fusion) | data formatting | bytes 16777216 | tf_op jit(solution)/shard_map/convert_element_type | solution.py:8
  468.9 8.9 %gather_fusion = bf16[64,128,512]{2,1,0:T(8,128)(2,1)} fusion(bf16[64,128,512]{2,1,0:T(8,128)(2,1)} %copy.14, s32[1024]{0:T(1024)S(1)} %pad_clamp_fusion), kind=kCustom, calls=%fused_computation.2 | custom fusion | bytes 16777472 | tf_op jit(solution)/shard_map/jit(_take)/gather | solution.py:18
  477.8 0.0 copy-start.1
  477.8 15.2 %fusion.4 = f32[64,128,128]{2,1,0:T(8,128)} fusion(bf16[64,128,512]{2,1,0:T(8,128)(2,1)} %gather_fusion, pred[64]{0:T(512)(128)(4,1)S(1)} %get-tuple-element.7, bf16[64,256,512]{2,1,0:T(8,128)(2,1)} %gather_fusion.1, pred[64]{0:T(512)(128)(4,1)S(1)} %get-tuple-element.6, bf16[1,64,256,128]{3,2,1,0:T(8,128)(2,1)} %param.12), kind=kOutput, calls=%fused_computation.8 | convolution fusion | flops 3238002688 | bytes 33554560 | tf_op jit(solution)/shard_map/pkq,plq->pkl/dot_general | solution.py:22
  493.0 0.0 reduce-scatter.2.cloned.1.call-update
  493.0 54.8 %reduce-scatter.2.cloned.1.call-done = f32[16,128,128]{2,1,0:T(8,128)} async-done(((f32[64,128,128]{2,1,0:T(8,128)}), f32[16,128,128]{2,1,0:T(8,128)}) %reduce-scatter.2.cloned.1.call-update) | async-done | bytes 1048592 | tf_op jit(solution)/shard_map/reduce_scatter | solution.py:21
  547.8 2.1 convert_bitcast_fusion.1
  549.9 0.0 copy-done.1
  (8 shorter events, 0.1 us)
Async XLA Ops:
  6.5 24.4 %copy-start = (bf16[4,256,512]{2,1,0:T(8,128)(2,1)S(1)}, bf16[4,256,512]{2,1,0:T(8,128)(2,1)}, u32[]{:S(2)}) copy-start(bf16[4,256,512]{2,1,0:T(8,128)(2,1)} %param.8) | copy-start | bytes 3145732
  75.0 6.2 %copy-start.3 = (s32[1,64]{1,0:T(1,128)S(1)}, s32[1,64]{1,0:T(1,128)}, u32[]{:S(2)}) copy-start(s32[1,64]{1,0:T(1,128)} %param.10) | copy-start | bytes 772
  75.0 370.6 %all-to-all-start.1 = ((bf16[64,256,512]{1,2,0:T(8,128)(2,1)}), bf16[64,256,512]{1,2,0:T(8,128)(2,1)}, u32[]{:S(2)}, u32[]{:S(2)}) async-start(bf16[64,256,512]{1,2,0:T(8,128)(2,1)} %broadcast_select_fusion), calls=%async_computation.1 | async-start | bytes 33554432 | tf_op jit(solution)/shard_map/all_to_all | solution.py:16
  81.0 466.8 %reduce-scatter.2.cloned.1.call-start = ((), (), s32[]{:S(2)}) async-start(), calls=%async_computation.3 | async-start | bytes 5242880 | tf_op jit(solution)/shard_map/reduce_scatter | solution.py:21
  81.3 7.5 %copy-start.2 = (s32[1,64]{1,0:T(1,128)S(1)}, s32[1,64]{1,0:T(1,128)}, u32[]{:S(2)}) copy-start(s32[1,64]{1,0:T(1,128)} %param.11) | copy-start | bytes 772
  477.8 72.2 %copy-start.1 = (bf16[4,256,512]{2,1,0:T(8,128)(2,1)S(1)}, bf16[4,256,512]{2,1,0:T(8,128)(2,1)}, u32[]{:S(2)}) copy-start(bf16[4,256,512]{2,1,0:T(8,128)(2,1)} %param.8) | copy-start | bytes 3145732
Sparse Core Ops, SparseCore 0:
  493.2 54.6 reduce-scatter.1
where the time goes:
time: 558 us; the launch traced here: 557 us
  waiting for transfers between devices  412 us (74%)
  local copies, waits for them, and re-layouts  59.1 us (11%)
  matrix products  26.5 us (5%)
  blocking collectives  22.3 us (4%)
  other arithmetic  17.5 us (3%)
  between operations  13.5 us (2%)
  starting transfers between devices  6.18 us (1%)
    all_to_all x1, waiting for transfers between devices, body(): lax.all_to_all(chosen, 'owner', split_axis=0, concat_axis=0, tiled=True)  357 us
    reduce_scatter x1, waiting for transfers between devices, body(): lax.psum_scatter(jnp.einsum('pkq,plq->pkl', left, right, preferred_elemen...  54.8 us
    gather x2, local copies, waits for them, and re-layouts, body(): chosen = jnp.take(blocks, served, axis=0)  29.9 us
    all_to_all x1, blocking collectives, body(): lax.all_to_all(wanted, 'owner', split_axis=1, concat_axis=0, tiled=True)  22.3 us
    dot_general x1, matrix products, body(): jnp.einsum('pkq,plq->pkl', left, right, preferred_element_type=jnp.float32)  15.2 us
    select_n x2, other arithmetic, body(): chosen = jnp.take(blocks, served, axis=0)  14.2 us
    convert_element_type x1, local copies, waits for them, and re-layouts, project(): jnp.einsum('pdk,pdq->pkq', maps, tiles, preferred_element_type=jnp.float32)  11.9 us
    dot_general x1, matrix products, project(): jnp.einsum('pdk,pdq->pkq', maps, tiles, preferred_element_type=jnp.float32)  11.3 us
  transfers between devices with their start and end apart: 2, of which 2 were waited for; matrix products, arithmetic and copies ran while one was open for 1% of the time, Pallas kernels for 0%

commit v1 on v0

v1 whole, which is shorter than its diff:
```python
import functools

import jax
import jax.numpy as jnp
from jax import lax
from jax.experimental import pallas as pl
from jax.experimental.pallas import tpu as pltpu
from jax.sharding import PartitionSpec as P

NX, NY, NZ = 4, 4, 8
PLANE = NY * 2
PAIRS = 64
BF16, F32, I32 = jnp.bfloat16, jnp.float32, jnp.int32
MESH = pl.DeviceIdType.MESH
OFFSETS = (0, -1, 1, -2, 2, -3, 3, 4)


def dot(a, b, ca, cb):
    return lax.dot_general(a, b, (((ca,), (cb,)), ((), ())), preferred_element_type=F32)


def kernel(
    blocks, pno_remote, pno_local, table, out,
    col0, col1, col2, col3, col4, col5, col6, col7,
    rows, maps, maps_local, tables, tables_s,
    stage_a, got_a, stage_b, got_b, acc, own, t_send, t_got, res,
    z_s, z_r, y_s, y_r, c_s, c_r, q_s, q_r, m_s, m_r, w_s, w_r,
    a_s, a_r, b_s, b_r, t_s, t_r, g_s, g_r, f_s, f_r, local_s,
):
    cols = (col0, col1, col2, col3, col4, col5, col6, col7)
    me = lax.axis_index("owner")
    x = lax.axis_index("aux")
    z = lax.div(me, PLANE)
    yc = lax.rem(me, PLANE)
    y = lax.div(yc, 2)
    c = lax.rem(yc, 2)

    def around(v, step, n):
        return lax.rem(v + (step + n), n)

    def at(zz, yy, cc):
        return (zz * NY + yy) * 2 + cc

    z_to = [(at(around(z, d, NZ), y, c), x) for d in (1, -1)]
    y_to = [(at(z, around(y, d, NY), c), x) for d in (1, -1)]
    x_to = [(me, around(x, d, NX)) for d in (1, -1)]
    mate = (at(z, y, 1 - c), x)
    peers = [
        (dy, dc, around(y, dy, NY) * 2 + lax.rem(c + dc, 2))
        for dy, dc in ((1, 0), (3, 0), (1, 1), (3, 1), (2, 0), (2, 1), (0, 1))
    ]

    barrier = pltpu.get_barrier_semaphore()
    hello = z_to + x_to + [(z * PLANE + p, x) for _, _, p in peers]
    for device in hello:
        pl.semaphore_signal(barrier, inc=1, device_id=device, device_id_type=MESH)
    pl.semaphore_wait(barrier, len(hello))

    sent = []

    def remote(src, dst, s, r, device):
        return pltpu.make_async_remote_copy(
            src_ref=src, dst_ref=dst, send_sem=s, recv_sem=r, device_id=device, device_id_type=MESH
        )

    def send(src, dst, s, r, device):
        copy = remote(src, dst, s, r, device)
        copy.start()
        sent.append(copy)

    def got(dst, s, r):
        remote(dst, dst, s, r, mate).wait_recv()

    stripe = pl.ds(pl.multiple_of(x * 64, 64), 64)

    local = []

    def copy_in(src, dst):
        copy = pltpu.make_async_copy(src, dst, local_s.at[len(local)])
        copy.start()
        local.append(copy)

    for n, (dy, dc, p) in enumerate(peers):
        send(table, tables.at[yc], w_s.at[n], w_r.at[n], (z * PLANE + p, x))
    for n, (dy, dc, p) in enumerate(peers):
        send(pno_remote.at[:, p, stripe], maps.at[yc, :, stripe], q_s.at[n], q_r.at[n], (z * PLANE + p, x))
    copy_in(pno_remote.at[:, yc, stripe], maps.at[yc, :, stripe])
    copy_in(table, tables.at[yc])
    copy_in(blocks, col0)
    copy_in(blocks, rows.at[yc])
    copy_in(pno_local, maps_local)

    def column(d, h):
        return 7 if h == 4 else 2 * h - 1 + d

    def orbitals(d, h):
        return range(4) if h < 4 else (range(2) if d == 0 else range(2, 4))

    def z_send(d, h, q):
        src = blocks if h == 1 else cols[column(d, h - 1)]
        send(src.at[q], cols[column(d, h)].at[q], z_s.at[d, h - 1, q], z_r.at[d, h - 1, q], z_to[d])

    def z_got(d, h, q):
        got(cols[column(d, h)].at[q], z_s.at[d, h - 1, q], z_r.at[d, h - 1, q])

    def y_from(d, h):
        return around(y, -h if d == 0 else h, NY) * 2 + c

    def y_send(d, h, q):
        src = blocks.at[q] if h == 1 else rows.at[y_from(d, 1), q]
        there = yc if h == 1 else y_from(d, 1)
        send(src, rows.at[there, q], y_s.at[d, h - 1, q], y_r.at[d, h - 1, q], y_to[d])

    def y_got(d, h, q):
        got(rows.at[y_from(d, h), q], y_s.at[d, h - 1, q], y_r.at[d, h - 1, q])

    def c_send(n, who, q):
        src = blocks.at[q] if n == 0 else rows.at[who, q]
        send(src, rows.at[who, q], c_s.at[n, q], c_r.at[n, q], mate)

    for q in range(4):
        for d in range(2):
            z_send(d, 1, q if d == 0 else 3 - q)
            y_send(d, 1, q if d == 0 else 3 - q)
    for q in range(4):
        c_send(0, yc, q)

    def m_half(d, h):
        return pl.ds(4 * h, 4)

    def m_send(d, hop, half):
        who = x if hop == 1 else around(x, -1 if d == 0 else 1, NX)
        there = maps.at[m_half(d, half), :, pl.ds(pl.multiple_of(who * 64, 64), 64)]
        send(there, there, m_s.at[d, hop - 1, half], m_r.at[d, hop - 1, half], x_to[d])

    def m_got(d, hop, half):
        who = around(x, -hop if d == 0 else hop, NX)
        got(
            maps.at[m_half(d, half), :, pl.ds(pl.multiple_of(who * 64, 64), 64)],
            m_s.at[d, hop - 1, half], m_r.at[d, hop - 1, half],
        )

    def peer_from(n):
        dy, dc, _ = peers[n]
        return around(y, -dy, NY) * 2 + lax.rem(c + dc, 2)

    for n in range(7):
        got(tables.at[peer_from(n)], w_s.at[n], w_r.at[n])
        got(maps.at[peer_from(n), :, stripe], q_s.at[n], q_r.at[n])
    for copy in local:
        copy.wait()
    for half in range(2):
        for d in range(2):
            m_send(d, 1, half if d == 0 else 1 - half)
    scalars = pltpu.make_async_copy(tables, tables_s, local_s.at[5])
    scalars.start()
    scalars.wait()

    def z_turn(h):
        for q in range(4):
            for d in range(2):
                o = q if d == 0 else 3 - q
                z_got(d, h, o)
                if o in orbitals(d, h + 1):
                    z_send(d, h + 1, o)

    z_turn(1)
    for q in range(4):
        for d in range(2):
            o = q if d == 0 else 3 - q
            y_got(d, 1, o)
            if q < 2:
                y_send(d, 2, o)
            c_send(1 + d, y_from(d, 1), o)
    for d in range(2):
        m_got(d, 1, d)
        m_send(d, 2, d)
    z_turn(2)
    for q in range(2):
        for d in range(2):
            o = q if d == 0 else 3 - q
            y_got(d, 2, o)
            c_send(3, y_from(d, 2), o)
    for d in range(2):
        m_got(d, 1, 1 - d)
        m_got(d, 2, d)
    for q in range(4):
        got(rows.at[y * 2 + 1 - c, q], c_s.at[0, q], c_r.at[0, q])
        for d in range(2):
            got(rows.at[around(y, -1 if d == 0 else 1, NY) * 2 + 1 - c, q], c_s.at[1 + d, q], c_r.at[1 + d, q])
        got(rows.at[around(y, 2, NY) * 2 + 1 - c, q], c_s.at[3, q], c_r.at[3, q])

    def plane(k):
        return around(z, OFFSETS[k], NZ)

    def row_of(k, dx):
        return lax.rem(x + (dx + 16) - y - plane(k), NY)

    def partial(k, dx, half):
        o = row_of(k, dx) * 2 + half
        s = plane(k) * PLANE + yc
        i = tables_s[o, 1, s]
        j = tables_s[o, 0, s]
        right = dot(maps[o, plane(k)], cols[k][j], 0, 0).astype(BF16)
        return dot(rows[o, i], right, 1, 1)

    def first(k):
        for half in range(2):
            stage_a[k, half] = partial(k, 2, half).astype(BF16)
            send(stage_a.at[k, half], got_a.at[k, half], a_s.at[k, half], a_r.at[k, half], x_to[half])
        for d in range(2):
            for half in (1 - d, d):
                part = partial(k, 3 if d else 1, half)
                if half == d:
                    acc[k, d] = part
                else:
                    stage_b[k, d, half] = part.astype(BF16)
                    b_send(k, d, half)
        for half in range(2):
            own[k, half] = partial(k, 0, half)

    def b_send(k, d, half):
        send(stage_b.at[k, d, half], got_b.at[k, d, half], b_s.at[k, d, half], b_r.at[k, d, half], x_to[d])

    def second(k):
        for d in range(2):
            got(got_a.at[k, d], a_s.at[k, d], a_r.at[k, d])
            stage_b[k, d, d] = (acc[k, d] + got_a[k, d].astype(F32)).astype(BF16)
            b_send(k, d, d)

    def t_copy(k, half):
        return remote(
            t_send.at[k, half], t_got.at[k, c], t_s.at[k, half], t_r.at[k, c], (at(z, row_of(k, 0), half), x)
        )

    def third(k):
        for half in range(2):
            for d in (0, 1):
                got(got_b.at[k, d, half], b_s.at[k, d, half], b_r.at[k, d, half])
            total = own[k, half] + got_b[k, 0, half].astype(F32) + got_b[k, 1, half].astype(F32)
            t_send[k, half] = total.astype(BF16)
            home = row_of(k, 0) * 2 + half == yc

            @pl.when(jnp.logical_not(home))
            def _():
                t_copy(k, half).start()

            @pl.when(home)
            def _():
                t_got[k, half] = t_send[k, half]

    def g_copy(k, d):
        pair = res.at[pl.ds(plane(k) * PLANE + row_of(k, 0) * 2, 2)]
        return pair

    def fourth(k):
        for half in range(2):
            home = row_of(k, 0) * 2 + half == yc

            @pl.when(jnp.logical_not(home))
            def _():
                got(t_got.at[k, half], t_s.at[k, half], t_r.at[k, half])

        s = plane(k) * PLANE + row_of(k, 0) * 2
        for half in range(2):
            p = tables_s[yc, 2, s + half]
            res[s + half] = dot(maps_local[p], t_got[k, half], 0, 0).astype(BF16)
        for d in range(2):
            there = res.at[pl.ds(s, 2)]
            send(there, there, g_s.at[k, d], g_r.at[k, d], x_to[d])

    def far(k, d, hop):
        dx = -hop if d == 0 else hop
        return plane(k) * PLANE + row_of(k, dx) * 2

    def fifth(k):
        for d in range(2):
            s = far(k, d, 1)
            got(res.at[pl.ds(s, 2)], g_s.at[k, d], g_r.at[k, d])
            send(res.at[s + d], res.at[s + d], f_s.at[k, d], f_r.at[k, d], x_to[d])

    def sixth(k):
        for d in range(2):
            got(res.at[far(k, d, 2) + d], f_s.at[k, d], f_r.at[k, d])

    steps = (first, second, third, fourth, fifth, sixth)

    def wave(front, lag_from, lag_to):
        for n in range(lag_from, lag_to):
            if 0 <= front - n < NZ:
                steps[n](front - n)

    for t in range(5):
        wave(t, 0, 6)
    z_turn(3)
    for t in range(5, 7):
        wave(t, 0, 6)
    for d in range(2):
        for o in orbitals(d, 4):
            z_got(d, 4, o)
    for t in range(7, NZ + 6):
        wave(t, 0, 6)

    def put(p, _):
        out[p] = res[tables_s[yc, 3, x * (PAIRS // NX) + p]]
        return 0

    lax.fori_loop(0, PAIRS // NX, put, 0)

    for copy in sent:
        copy.wait_send()
    for k in range(NZ):
        for half in range(2):
            home = row_of(k, 0) * 2 + half == yc

            @pl.when(jnp.logical_not(home))
            def _():
                t_copy(k, half).wait_send()


def body(blocks, wanted, pair_local, pair_slot, pno_local, pno_remote):
    dom, slab = blocks.shape[1:]
    npno = pno_local.shape[-1]
    slot = pair_slot.reshape(PAIRS, 1)
    hit = (slot == jnp.arange(PAIRS, dtype=I32)[None, :]).astype(I32)
    first = jnp.sum(hit * pair_local.reshape(PAIRS, 1), axis=0)
    place = jnp.sum(hit * jnp.arange(PAIRS, dtype=I32)[:, None], axis=0)
    lines = jnp.stack([wanted.reshape(PAIRS), first, place, pair_slot.reshape(PAIRS)])
    table = jnp.pad(lines, ((0, 4), (0, 128 - PAIRS)))

    dma = pltpu.SemaphoreType.DMA
    square = (dom, npno)
    call = pl.pallas_call(
        kernel,
        out_shape=jax.ShapeDtypeStruct((PAIRS // NX, npno, npno), BF16),
        in_specs=[pl.BlockSpec(memory_space=pl.ANY)] * 4,
        out_specs=pl.BlockSpec(memory_space=pltpu.VMEM),
        scratch_shapes=[pltpu.VMEM((4, dom, slab), BF16)] * NZ
        + [
            pltpu.VMEM((PLANE, 4, dom, slab), BF16),
            pltpu.VMEM((PLANE, NZ) + square, BF16),
            pltpu.VMEM((PAIRS,) + square, BF16),
            pltpu.VMEM((PLANE, 8, 128), I32),
            pltpu.SMEM((PLANE, 8, 128), I32),
            pltpu.VMEM((NZ, 2) + square, BF16),
            pltpu.VMEM((NZ, 2) + square, BF16),
            pltpu.VMEM((NZ, 2, 2) + square, BF16),
            pltpu.VMEM((NZ, 2, 2) + square, BF16),
            pltpu.VMEM((NZ, 2) + square, F32),
            pltpu.VMEM((NZ, 2) + square, F32),
            pltpu.VMEM((NZ, 2) + square, BF16),
            pltpu.VMEM((NZ, 2) + square, BF16),
            pltpu.VMEM((PAIRS, npno, npno), BF16),
            dma((2, 4, 4)), dma((2, 4, 4)),
            dma((2, 2, 4)), dma((2, 2, 4)),
            dma((4, 4)), dma((4, 4)),
            dma((7,)), dma((7,)),
            dma((2, 2, 2)), dma((2, 2, 2)),
            dma((7,)), dma((7,)),
            dma((NZ, 2)), dma((NZ, 2)),
            dma((NZ, 2, 2)), dma((NZ, 2, 2)),
            dma((NZ, 2)), dma((NZ, 2)),
            dma((NZ, 2)), dma((NZ, 2)),
            dma((NZ, 2)), dma((NZ, 2)),
            dma((6,)),
        ],
        compiler_params=pltpu.CompilerParams(
            collective_id=0, has_side_effects=True, vmem_limit_bytes=56 * 1024 * 1024
        ),
        cost_estimate=pl.CostEstimate(
            flops=4 * PAIRS * dom * slab * npno, bytes_accessed=1 << 24, transcendentals=0
        ),
    )
    maps = pno_remote.reshape(NZ, PLANE, dom, npno)
    return call(blocks, maps, pno_local.reshape(PAIRS, dom, npno), table)[None]


def solution(mesh):
    in_specs = (
        P("owner", None, "aux"),
        P("owner", None, None),
        P("owner", None),
        P("owner", None),
        P("owner", None, None, None),
        P("owner", None, None, None),
    )
    out_specs = P("owner", "aux", None, None)
    return jax.shard_map(body, mesh=mesh, in_specs=in_specs, out_specs=out_specs, check_vma=False)
```

time: 558 us -> 125 us (0.22)
  waiting for transfers between devices: 412 us -> 0 us
  Pallas kernels: 0 us -> 121 us
  local copies, waits for them, and re-layouts: 59.1 us -> 2.48 us
  matrix products: 26.5 us -> 0 us
  blocking collectives: 22.3 us -> 0 us
  other arithmetic: 17.5 us -> 1.45 us
  between operations: 13.5 us -> 0.01 us
  starting transfers between devices: 6.18 us -> 0 us
    all_to_all x1 -> x0, waiting for transfers between devices: 357 us -> none  [body(): lax.all_to_all(chosen, 'owner', split_axis=0, concat_axis=0, tiled=True)]
    pallas_call x0 -> x1, Pallas kernels: none -> 121 us  [body(): return call(blocks, maps, pno_local.reshape(PAIRS, dom, npno), table)[None]]
    reduce_scatter x1 -> x0, waiting for transfers between devices: 54.8 us -> none  [body(): lax.psum_scatter(jnp.einsum('pkq,plq->pkl', left, right, preferred_elemen...]
    gather x4 -> x0, local copies, waits for them, and re-layouts: 46.3 us -> none  [the longest x2 29.9 us: body(): chosen = jnp.take(blocks, served, axis=0)]
    dot_general x2 -> x0, matrix products: 26.5 us -> none  [the longest x1 15.2 us: body(): jnp.einsum('pkq,plq->pkl', left, right, preferred_element_type=jnp.float32)]
    all_to_all x1 -> x0, blocking collectives: 22.3 us -> none  [body(): lax.all_to_all(wanted, 'owner', split_axis=1, concat_axis=0, tiled=True)]
    select_n x4 -> x0, other arithmetic: 14.2 us -> none  [the longest x2 14.2 us: body(): chosen = jnp.take(blocks, served, axis=0)]
    convert_element_type x1 -> x0, local copies, waits for them, and re-layouts: 11.9 us -> none  [project(): jnp.einsum('pdk,pdq->pkq', maps, tiles, preferred_element_type=jnp.float32)]
  transfers between devices with their start and end apart: 2 -> 0, of which waited for: 2 -> 0; matrix products, arithmetic and copies ran while one was open for 1% -> 0% of each run, Pallas kernels for 0% -> 0%
where the time goes in v1:
time: 125 us
  Pallas kernels  121 us (97%)
  local copies, waits for them, and re-layouts  2.48 us (2%)
  other arithmetic  1.45 us (1%)
    pallas_call x1, Pallas kernels, body(): return call(blocks, maps, pno_local.reshape(PAIRS, dom, npno), table)[None]  121 us

profile of v1, /device:TPU:1, one launch (start us, length us, event | category | flops | bytes accessed | tf_op | source)
XLA Modules:
  0.0 125.3 jit_solution(13133409853366736944)
XLA Ops:
  0.0 0.8 select_reduce_fusion.1
  0.8 0.7 pad_add_fusion
  1.5 0.6 pad.4.table
  2.1 121.3 %shard_map.64 = bf16[16,128,128]{2,1,0:T(8,128)(2,1)} custom-call(bf16[4,256,512]{2,1,0:T(8,128)(2,1)} %blocks.1, bf16[8,8,256,128]{3,2,1,0:T(8,128)(2,1)} %bitcast.14, bf16[64,256,128]{2,1,0:T(8,128)(2,1)} %bitcast.15, s32[8,128]{1,0:T(8,128)} %pad.4.table), custom_call_target="tpu_custom_call" | custom-call | flops 4294967296 | bytes 16777216 | tf_op jit(solution)/shard_map/pallas_call | solution.py:375
  123.4 1.9 %copy.8 = bf16[1,16,128,128]{3,2,1,0:T(8,128)(2,1)} copy(bf16[1,16,128,128]{3,2,1,0:T(8,128)(2,1)} %bitcast.8) | data formatting | bytes 1048576

commit v2 on v0

v2 whole, which is shorter than its diff:
```python
import jax
import jax.numpy as jnp
from jax import lax
from jax.experimental import pallas as pl
from jax.experimental.pallas import tpu as pltpu
from jax.sharding import PartitionSpec as P

NX, NY, NZ = 4, 4, 8
PLANE = NY * 2
PAIRS = 64
BF16, F32, I32 = jnp.bfloat16, jnp.float32, jnp.int32
MESH = pl.DeviceIdType.MESH
OFFSETS = (0, -1, 1, -2, 2, -3, 3, 4)
STRIPE, PART = 64, 32
UNITS = (
    (0, 1, 0, 3, 3.35),
    (1, 2, 0, 3, 3.4),
    (2, 3, 0, 3, 3.55),
    (0, 3, 3, 4, 4.15),
    (3, 4, 0, 4, 4.55),
    (4, 5, 0, 4, 5.05),
    (5, 6, 0, 4, 6.05),
    (6, 7, 0, 4, 6.1),
    (7, 8, 0, 4, 7.05),
)
LAST = len(UNITS) - 1
LATER = (
    (6.2, 0, 7), (6.25, 1, 6), (6.26, 2, 5), (7.06, 2, 6), (7.07, 1, 7), (7.08, 2, 7), (7.1, 1, 8), (7.11, 2, 8),
)
DIRECT = (LAST,)


def dot(a, b, ca, cb):
    return lax.dot_general(a, b, (((ca,), (cb,)), ((), ())), preferred_element_type=F32)


def kernel(
    blocks, pno_remote, pno_local, table, final,
    col0, col1, col2, col3, col4, col5, col6, col7,
    rows0, rows1, rows2, rows3, maps, maps_local, tables, tables_s,
    stage_a, got_a, stage_b, got_b, acc, own, t_send, t_got, tmp, res, picked,
    z_s, z_r, y_s, y_r, c_s, c_r, q_s, q_r, m_s, m_r, n_s, n_r, w_s, w_r,
    a_s, a_r, b_s, b_r, t_s, t_r, f_s, f_r, local_s,
):
    rows = (rows0, rows1, rows2, rows3)
    cols = (col0, col1, col2, col3, col4, col5, col6, col7)
    me = lax.axis_index("owner")
    x = lax.axis_index("aux")
    z = lax.div(me, PLANE)
    yc = lax.rem(me, PLANE)
    y = lax.div(yc, 2)
    c = lax.rem(yc, 2)

    def around(v, step, n):
        return lax.rem(v + (step + n), n)

    def at(zz, yy, cc):
        return (zz * NY + yy) * 2 + cc

    z_to = [(at(around(z, d, NZ), y, c), x) for d in (1, -1)]
    y_to = [(at(z, around(y, d, NY), c), x) for d in (1, -1)]
    x_to = [(me, around(x, d, NX)) for d in (1, -1)]
    x_far = (me, around(x, 2, NX))
    mate = (at(z, y, 1 - c), x)
    turns = [(dy, dc) for dy in (0, -1, 1, 2) for dc in (0, 1)]
    peers = [around(y, dy, NY) * 2 + lax.rem(c + dc, 2) for dy, dc in turns]
    whose = [around(y, -dy, NY) * 2 + lax.rem(c + dc, 2) for dy, dc in turns]

    def plane(k):
        return around(z, OFFSETS[k], NZ)

    barrier = pltpu.get_barrier_semaphore()
    hello = z_to + x_to + [x_far] + [(z * PLANE + p, x) for p in peers[1:]]
    for device in hello:
        pl.semaphore_signal(barrier, inc=1, device_id=device, device_id_type=MESH)
    pl.semaphore_wait(barrier, len(hello))

    sent = []

    def remote(src, dst, s, r, device):
        return pltpu.make_async_remote_copy(
            src_ref=src, dst_ref=dst, send_sem=s, recv_sem=r, device_id=device, device_id_type=MESH
        )

    def send(src, dst, s, r, device):
        copy = remote(src, dst, s, r, device)
        copy.start()
        sent.append(copy)

    def got(dst, s, r):
        remote(dst, dst, s, r, mate).wait_recv()

    local = []

    def copy_in(src, dst):
        copy = pltpu.make_async_copy(src, dst, local_s.at[len(local)])
        copy.start()
        local.append(copy)

    def column(d, h):
        return 7 if h == 4 else 2 * h - 1 + d

    def orbitals(d, h):
        return range(4) if h < 4 else (range(2) if d == 0 else range(2, 4))

    def z_send(d, h, q):
        src = blocks if h == 1 else cols[column(d, h - 1)]
        send(src.at[q], cols[column(d, h)].at[q], z_s.at[d, h - 1, q], z_r.at[d, h - 1, q], z_to[d])

    def z_got(d, h, q):
        got(cols[column(d, h)].at[q], z_s.at[d, h - 1, q], z_r.at[d, h - 1, q])

    def y_send(d, h, q):
        src = blocks.at[q] if h == 1 else rows[1 + d].at[c, q]
        dst = rows[1 + d] if h == 1 else rows[3]
        send(src, dst.at[c, q], y_s.at[d, h - 1, q], y_r.at[d, h - 1, q], y_to[d])

    def y_got(d, h, q):
        got((rows[1 + d] if h == 1 else rows[3]).at[c, q], y_s.at[d, h - 1, q], y_r.at[d, h - 1, q])

    def c_send(m, q):
        src = blocks if m == 0 else rows[m].at[c]
        send(src.at[q], rows[m].at[c, q], c_s.at[m, q], c_r.at[m, q], mate)

    def stripe_of(who):
        return pl.ds(pl.multiple_of(who * STRIPE, STRIPE), STRIPE)

    stripe = stripe_of(x)

    def q_send(n):
        src = pno_remote.at[:, peers[n], stripe]
        send(src, maps.at[yc, :, stripe], q_s.at[n], q_r.at[n], (z * PLANE + peers[n], x))

    def m_ref(n, who):
        return maps.at[whose[n], :, stripe_of(who)]

    def m_send(n, d):
        there = m_ref(n, x)
        send(there, there, m_s.at[d, n], m_r.at[d, n], x_to[d])

    def m_turn(n, d):
        there = m_ref(n, around(x, -1 if d == 0 else 1, NX))
        got(there, m_s.at[d, n], m_r.at[d, n])
        if n % 2 == d:
            send(there, there, n_s.at[d, n], n_r.at[d, n], x_to[d])

    def m_last(n):
        d = n % 2
        got(m_ref(n, around(x, -2 if d == 0 else 2, NX)), n_s.at[d, n], n_r.at[d, n])

    for n in range(2):
        for d in range(2):
            z_send(d, 1, n if d == 0 else 3 - n)
    copy_in(pno_remote.at[:, yc, stripe], maps.at[yc, :, stripe])
    for n in range(1, PLANE - 2):
        q_send(n)
    for n in range(2):
        for d in range(2):
            y_send(d, 1, n if d == 0 else 3 - n)
    local[0].wait()
    for d in range(2):
        m_send(0, d)
    for q in range(4):
        c_send(0, q)

    for n in range(1, PLANE):
        send(table, tables.at[yc], w_s.at[n], w_r.at[n], (z * PLANE + peers[n], x))

    first_local = len(local)
    copy_in(table, tables.at[yc])
    copy_in(blocks, col0)
    copy_in(blocks, rows0.at[c])
    copy_in(pno_local, maps_local)

    def w_turn():
        for n in range(1, PLANE):
            got(tables.at[whose[n]], w_s.at[n], w_r.at[n])
        for copy in local[first_local:]:
            copy.wait()
        scalars = pltpu.make_async_copy(tables, tables_s, local_s.at[len(local)])
        scalars.start()
        scalars.wait()

    def q_turn(n):
        got(maps.at[whose[n], :, stripe], q_s.at[n], q_r.at[n])
        for d in range(2):
            m_send(n, d)

    def z_turn(d, h, o, n):
        z_got(d, h, o)
        if h == 1 and n < 2:
            z_send(d, 1, o + 2 if d == 0 else o - 2)
        if h < 4 and o in orbitals(d, h + 1):
            z_send(d, h + 1, o)

    def y_turn(d, h, o, n):
        y_got(d, h, o)
        if h == 1 and n < 2:
            y_send(d, 1, o + 2 if d == 0 else o - 2)
        if h == 1 and n >= 2:
            y_send(d, 2, o - 2 if d == 0 else o + 2)
        c_send(1 + d if h == 1 else 3, o)

    def c_turn(*which):
        for m in which:
            for q in range(4):
                got(rows[m].at[1 - c, q], c_s.at[m, q], c_r.at[m, q])

    def part_of(dx):
        return pl.ds(pl.multiple_of(around(x, dx, NX) * PART, PART), PART)

    def partial(k, n):
        s = plane(k) * PLANE + yc
        i = tables_s[peers[n], 1, s]
        j = tables_s[peers[n], 0, s]
        right = dot(maps[peers[n], plane(k)], cols[k][j], 0, 0).astype(BF16)
        return dot(right, rows[n // 2][around(c, n % 2, 2), i], 1, 1)

    def share_of(u):
        k, k_end, m, m_end, _ = UNITS[u]
        return pl.ds(k, k_end - k), pl.ds(m, m_end - m)

    def b_ref(ref, u, d, half):
        ks, ms = share_of(u)
        return ref.at[ks, d, half, ms]

    def b_send(u, d, half):
        send(b_ref(stage_b, u, d, half), b_ref(got_b, u, d, half), b_s.at[u, d, half], b_r.at[u, d, half], x_to[d])

    def a_ref(ref, u, half):
        ks, ms = share_of(u)
        return ref.at[ks, half, ms]

    def first(u):
        k0, k1, m0, m1, _ = UNITS[u]
        for k in range(k0, k1):
            for n in range(2 * m0, 2 * m1):
                half, m = n % 2, n // 2
                tmp[half] = partial(k, n)
                stage_a[k, half, m] = tmp[half, part_of(2)].astype(BF16)
                for d in range(2):
                    part = tmp[half, part_of(-1 if d else 1)]
                    if half == d and u not in DIRECT:
                        acc[k, d, m] = part
                    else:
                        stage_b[k, d, half, m] = part.astype(BF16)
                own[k, half, m] = tmp[half, part_of(0)]
        for half in range(2):
            device = x_far if u in DIRECT else x_to[half]
            send(a_ref(stage_a, u, half), a_ref(got_a, u, half), a_s.at[u, half], a_r.at[u, half], device)
        for d in range(2):
            b_send(u, d, 1 - d)
            if u in DIRECT:
                b_send(u, d, d)

    def second(u):
        if u in DIRECT:
            return
        k0, k1, m0, m1, _ = UNITS[u]
        for d in range(2):
            got(a_ref(got_a, u, d), a_s.at[u, d], a_r.at[u, d])
            for k in range(k0, k1):
                for m in range(m0, m1):
                    stage_b[k, d, d, m] = (acc[k, d, m] + got_a[k, d, m].astype(F32)).astype(BF16)
            b_send(u, d, d)

    def b_wait(u):
        for half in range(2):
            for d in range(2):
                got(b_ref(got_b, u, d, half), b_s.at[u, d, half], b_r.at[u, d, half])
            if u in DIRECT:
                got(a_ref(got_a, u, half), a_s.at[u, half], a_r.at[u, half])

    def third(k):
        for half in range(2):
            total = own[k, half]
            for d in range(2):
                total = total + got_b[k, d, half].astype(F32)
            if LAST in DIRECT and k == NZ - 1:
                total = total + got_a[k, half].astype(F32)
            t_send[k, half] = total.astype(BF16)
            for m in range(NY):
                n = 2 * m + half
                if n == 0:
                    t_got[k, yc] = t_send[k, 0, 0]
                else:
                    send(
                        t_send.at[k, half, m], t_got.at[k, yc], t_s.at[k, n], t_r.at[k, n],
                        (z * PLANE + peers[n], x),
                    )

    def fourth(k):
        for n in range(PLANE):
            if n:
                got(t_got.at[k, whose[n]], t_s.at[k, n], t_r.at[k, n])
            s = plane(k) * PLANE + whose[n]
            p = tables_s[yc, 2, s]
            res[s] = dot(t_got[k, whose[n]], maps_local[p], 1, 0).astype(BF16)

    def thirds(u):
        b_wait(u)
        if u == 3:
            for k in range(3):
                third(k)
        elif u > 3:
            third(UNITS[u][0])

    def fourths(u):
        for k in range(3) if u == 3 else range(UNITS[u][0], UNITS[u][1]) if u > 3 else ():
            fourth(k)

    events = []

    def when(time, what, *args):
        events.append((time, len(events), what, args))

    for n in range(4):
        for d in range(2):
            o = n if d == 0 else 3 - n
            for h in (1, 2, 3):
                when(2 * (h - 1) + 0.5 * (n + 1), z_turn, d, h, o, n)
            when(1 + 0.5 * (n + 1), y_turn, d, 1, o, n)
            if n < 2:
                when(3 + 0.5 * (n + 1), y_turn, d, 2, o, n)
                when(6.5 + 0.5 * n, z_turn, d, 4, o, n)
    when(1.1, w_turn)
    for n in range(PLANE):
        if n:
            when(0.4 + 0.1 * n if n < 6 else 1.2 + 0.1 * n, q_turn, n)
        for d in range(2):
            when(0.75 + 0.33 * n, m_turn, n, d)
        when(1.3 + 0.33 * n, m_last, n)
    for n in range(PLANE - 2, PLANE):
        when(0.97, q_send, n)
    when(1.6, c_turn, 0)
    when(3.3, c_turn, 1, 2)
    when(4.1, c_turn, 3)
    begin = [unit[-1] for unit in UNITS]
    for u in range(LAST + 1):
        when(begin[u], first, u)
        for after, what in enumerate((second, thirds, fourths), start=1):
            if u + after < 8:
                when(begin[u + after] + 0.001 * after, what, u)
    for time, what, u in LATER:
        when(time, (second, thirds, fourths)[what], u)
    for _, _, what, args in sorted(events, key=lambda e: e[:2]):
        what(*args)

    share = PAIRS // NX
    for dx in (2, 1, 3, 0):
        def pick(p, _):
            picked[dx, p] = res[tables_s[yc, 3, around(x, dx, NX) * share + p]]
            return 0

        lax.fori_loop(0, share, pick, 0)
        if dx:
            device = (me, around(x, dx, NX))
            send(picked.at[dx], final.at[:, part_of(0)], f_s.at[dx], f_r.at[dx], device)
        else:
            final[:, part_of(0)] = picked[0]
    for dx in (1, 3, 2):
        got(final.at[:, part_of(-dx)], f_s.at[dx], f_r.at[dx])

    for copy in sent:
        copy.wait_send()


def body(blocks, wanted, pair_local, pair_slot, pno_local, pno_remote):
    dom, slab = blocks.shape[1:]
    npno = pno_local.shape[-1]
    dma = pltpu.SemaphoreType.DMA
    square, strip = (dom, npno), (PART, dom)

    def pair_of(*shape):
        return [dma(shape), dma(shape)]

    call = pl.pallas_call(
        kernel,
        out_shape=jax.ShapeDtypeStruct((PAIRS // NX, npno, npno), BF16),
        in_specs=[pl.BlockSpec(memory_space=pl.ANY)] * 4,
        out_specs=pl.BlockSpec(memory_space=pltpu.VMEM),
        scratch_shapes=[pltpu.VMEM((4, dom, slab), BF16)] * NZ
        + [pltpu.VMEM((2, 4, dom, slab), BF16)] * NY
        + [
            pltpu.VMEM((PLANE, NZ) + square, BF16),
            pltpu.VMEM((PAIRS,) + square, BF16),
            pltpu.VMEM((PLANE, 8, 128), I32),
            pltpu.SMEM((PLANE, 8, 128), I32),
            pltpu.VMEM((NZ, 2, NY) + strip, BF16),
            pltpu.VMEM((NZ, 2, NY) + strip, BF16),
            pltpu.VMEM((NZ, 2, 2, NY) + strip, BF16),
            pltpu.VMEM((NZ, 2, 2, NY) + strip, BF16),
            pltpu.VMEM((NZ, 2, NY) + strip, F32),
            pltpu.VMEM((NZ, 2, NY) + strip, F32),
            pltpu.VMEM((NZ, 2, NY) + strip, BF16),
            pltpu.VMEM((NZ, PLANE) + strip, BF16),
            pltpu.VMEM((2, npno, dom), F32),
            pltpu.VMEM((PAIRS, PART, npno), BF16),
            pltpu.VMEM((NX, PAIRS // NX, PART, npno), BF16),
        ]
        + pair_of(2, 4, 4)
        + pair_of(2, 2, 4)
        + pair_of(4, 4)
        + pair_of(PLANE)
        + pair_of(2, PLANE)
        + pair_of(2, PLANE)
        + pair_of(PLANE)
        + pair_of(LAST + 1, 2)
        + pair_of(LAST + 1, 2, 2)
        + pair_of(NZ, PLANE)
        + pair_of(NX)
        + [dma((6,))],
        compiler_params=pltpu.CompilerParams(
            collective_id=0, has_side_effects=True, vmem_limit_bytes=56 * 1024 * 1024
        ),
        cost_estimate=pl.CostEstimate(
            flops=4 * PAIRS * dom * slab * npno, bytes_accessed=1 << 24, transcendentals=0
        ),
    )
    maps = pno_remote.reshape(NZ, PLANE, dom, npno)
    slot = pair_slot.reshape(PAIRS, 1)
    hit = (slot == jnp.arange(PAIRS, dtype=I32)[None, :]).astype(I32)
    first = jnp.sum(hit * pair_local.reshape(PAIRS, 1), axis=0)
    place = jnp.sum(hit * jnp.arange(PAIRS, dtype=I32)[:, None], axis=0)
    lines = jnp.stack([wanted.reshape(PAIRS), first, place, pair_slot.reshape(PAIRS)])
    table = jnp.pad(lines, ((0, 4), (0, 128 - PAIRS)))
    turned = call(blocks, maps, pno_local.reshape(PAIRS, dom, npno), table)
    return jnp.swapaxes(turned, 1, 2)[None]


def solution(mesh):
    in_specs = (
        P("owner", None, "aux"),
        P("owner", None, None),
        P("owner", None),
        P("owner", None),
        P("owner", None, None, None),
        P("owner", None, None, None),
    )
    out_specs = P("owner", "aux", None, None)
    return jax.shard_map(body, mesh=mesh, in_specs=in_specs, out_specs=out_specs, check_vma=False)
```

time: 558 us -> 123 us (0.22)
  waiting for transfers between devices: 412 us -> 0 us
  Pallas kernels: 0 us -> 119 us
  local copies, waits for them, and re-layouts: 59.1 us -> 2.64 us
  matrix products: 26.5 us -> 0 us
  blocking collectives: 22.3 us -> 0 us
  other arithmetic: 17.5 us -> 1.45 us
  between operations: 13.5 us -> 0.01 us
  starting transfers between devices: 6.18 us -> 0 us
    all_to_all x1 -> x0, waiting for transfers between devices: 357 us -> none  [body(): lax.all_to_all(chosen, 'owner', split_axis=0, concat_axis=0, tiled=True)]
    pallas_call x0 -> x1, Pallas kernels: none -> 119 us  [body(): turned = call(blocks, maps, pno_local.reshape(PAIRS, dom, npno), table)]
    reduce_scatter x1 -> x0, waiting for transfers between devices: 54.8 us -> none  [body(): lax.psum_scatter(jnp.einsum('pkq,plq->pkl', left, right, preferred_elemen...]
    gather x4 -> x0, local copies, waits for them, and re-layouts: 46.3 us -> none  [the longest x2 29.9 us: body(): chosen = jnp.take(blocks, served, axis=0)]
    dot_general x2 -> x0, matrix products: 26.5 us -> none  [the longest x1 15.2 us: body(): jnp.einsum('pkq,plq->pkl', left, right, preferred_element_type=jnp.float32)]
    all_to_all x1 -> x0, blocking collectives: 22.3 us -> none  [body(): lax.all_to_all(wanted, 'owner', split_axis=1, concat_axis=0, tiled=True)]
    select_n x4 -> x0, other arithmetic: 14.2 us -> none  [the longest x2 14.2 us: body(): chosen = jnp.take(blocks, served, axis=0)]
    convert_element_type x1 -> x0, local copies, waits for them, and re-layouts: 11.9 us -> none  [project(): jnp.einsum('pdk,pdq->pkq', maps, tiles, preferred_element_type=jnp.float32)]
  transfers between devices with their start and end apart: 2 -> 0, of which waited for: 2 -> 0; matrix products, arithmetic and copies ran while one was open for 1% -> 0% of each run, Pallas kernels for 0% -> 0%
where the time goes in v2:
time: 123 us
  Pallas kernels  119 us (97%)
  local copies, waits for them, and re-layouts  2.64 us (2%)
  other arithmetic  1.45 us (1%)
    pallas_call x1, Pallas kernels, body(): turned = call(blocks, maps, pno_local.reshape(PAIRS, dom, npno), table)  119 us

profile of v2, /device:TPU:1, one launch (start us, length us, event | category | flops | bytes accessed | tf_op | source)
XLA Modules:
  0.0 122.6 jit_solution(5668315677815308951)
XLA Ops:
  0.0 0.8 select_reduce_fusion.1
  0.8 0.7 pad_add_fusion
  1.5 0.6 pad.4.table
  2.1 118.5 %shard_map.64 = bf16[16,128,128]{2,1,0:T(8,128)(2,1)} custom-call(bf16[4,256,512]{2,1,0:T(8,128)(2,1)} %blocks.1, bf16[8,8,256,128]{3,2,1,0:T(8,128)(2,1)} %bitcast.16, bf16[64,256,128]{2,1,0:T(8,128)(2,1)} %bitcast.17, s32[8,128]{1,0:T(8,128)} %pad.4.table), custom_call_target="tpu_custom_call" | custom-call | flops 4294967296 | bytes 16777216 | tf_op jit(solution)/shard_map/pallas_call | solution.py:427
  120.6 2.0 %copy.8 = bf16[1,16,128,128]{3,2,1,0:T(8,128)(2,1)} copy(bf16[1,16,128,128]{2,3,1,0:T(8,128)(2,1)} %bitcast.10) | data formatting | bytes 1048576 | tf_op jit(solution)/shard_map/broadcast_in_dim | solution.py:428

commit v3 on v2

--- a/solution.py
+++ b/solution.py
@@ -25,7 +25,7 @@
 )
 LAST = len(UNITS) - 1
 LATER = (
-    (6.2, 0, 7), (6.25, 1, 6), (6.26, 2, 5), (7.06, 2, 6), (7.07, 1, 7), (7.08, 2, 7), (7.1, 1, 8), (7.11, 2, 8),
+    (6.2, 0, 7), (6.25, 1, 6), (6.26, 2, 5), (7.06, 2, 6), (7.07, 1, 7), (7.1, 1, 8), (7.105, 2, 7), (7.11, 2, 8),
 )
 DIRECT = (LAST,)
 
@@ -35,9 +35,9 @@
 
 
 def kernel(
-    blocks, pno_remote, pno_local, table, final,
+    blocks, pno_remote, pno_local, wanted, pair_local, pair_slot, final,
     col0, col1, col2, col3, col4, col5, col6, col7,
-    rows0, rows1, rows2, rows3, maps, maps_local, tables, tables_s,
+    rows0, rows1, rows2, rows3, maps, maps_local, table, tables, tables_s,
     stage_a, got_a, stage_b, got_b, acc, own, t_send, t_got, tmp, res, picked,
     z_s, z_r, y_s, y_r, c_s, c_r, q_s, q_r, m_s, m_r, n_s, n_r, w_s, w_r,
     a_s, a_r, b_s, b_r, t_s, t_r, f_s, f_r, local_s,
@@ -163,6 +163,19 @@
     for q in range(4):
         c_send(0, q)
 
+    ones = lax.broadcasted_iota(I32, (PAIRS, PAIRS), 0)
+    lanes = lax.broadcasted_iota(I32, (PAIRS, PAIRS), 1)
+    eye = (ones == lanes).astype(F32)
+    slot = jnp.sum(eye * pair_slot[...].astype(F32), axis=1, keepdims=True)
+    start = jnp.sum(eye * pair_local[...].astype(F32), axis=1, keepdims=True)
+    hit = (slot.astype(I32) == lanes).astype(F32)
+    table[...] = jnp.zeros_like(table)
+    table[0:1, 0:PAIRS] = wanted[...]
+    table[1:2, 0:PAIRS] = jnp.clip(jnp.max(hit * start, axis=0, keepdims=True).astype(I32), 0, 3)
+    table[2:3, 0:PAIRS] = jnp.clip(
+        jnp.max(hit * ones.astype(F32), axis=0, keepdims=True).astype(I32), 0, PAIRS - 1
+    )
+    table[3:4, 0:PAIRS] = pair_slot[...]
     for n in range(1, PLANE):
         send(table, tables.at[yc], w_s.at[n], w_r.at[n], (z * PLANE + peers[n], x))
 
@@ -377,13 +390,14 @@
     call = pl.pallas_call(
         kernel,
         out_shape=jax.ShapeDtypeStruct((PAIRS // NX, npno, npno), BF16),
-        in_specs=[pl.BlockSpec(memory_space=pl.ANY)] * 4,
+        in_specs=[pl.BlockSpec(memory_space=pl.ANY)] * 3 + [pl.BlockSpec(memory_space=pltpu.VMEM)] * 3,
         out_specs=pl.BlockSpec(memory_space=pltpu.VMEM),
         scratch_shapes=[pltpu.VMEM((4, dom, slab), BF16)] * NZ
         + [pltpu.VMEM((2, 4, dom, slab), BF16)] * NY
         + [
             pltpu.VMEM((PLANE, NZ) + square, BF16),
             pltpu.VMEM((PAIRS,) + square, BF16),
+            pltpu.VMEM((8, 128), I32),
             pltpu.VMEM((PLANE, 8, 128), I32),
             pltpu.SMEM((PLANE, 8, 128), I32),
             pltpu.VMEM((NZ, 2, NY) + strip, BF16),
@@ -418,13 +432,9 @@
         ),
     )
     maps = pno_remote.reshape(NZ, PLANE, dom, npno)
-    slot = pair_slot.reshape(PAIRS, 1)
-    hit = (slot == jnp.arange(PAIRS, dtype=I32)[None, :]).astype(I32)
-    first = jnp.sum(hit * pair_local.reshape(PAIRS, 1), axis=0)
-    place = jnp.sum(hit * jnp.arange(PAIRS, dtype=I32)[:, None], axis=0)
-    lines = jnp.stack([wanted.reshape(PAIRS), first, place, pair_slot.reshape(PAIRS)])
-    table = jnp.pad(lines, ((0, 4), (0, 128 - PAIRS)))
-    turned = call(blocks, maps, pno_local.reshape(PAIRS, dom, npno), table)
+    turned = call(
+        blocks, maps, pno_local.reshape(PAIRS, dom, npno), wanted.reshape(1, PAIRS), pair_local, pair_slot
+    )
     return jnp.swapaxes(turned, 1, 2)[None]
 
 

time: 123 us -> 121 us (0.984)
  other arithmetic: 1.45 us -> 0 us
where the time goes in v3:
time: 121 us
  Pallas kernels  119 us (98%)
  local copies, waits for them, and re-layouts  2.04 us (2%)
    pallas_call x1, Pallas kernels, body(): call(blocks, maps, pno_local.reshape(PAIRS, dom, npno), wanted.reshape(1,...  119 us

profile of v3, /device:TPU:1, one launch (start us, length us, event | category | flops | bytes accessed | tf_op | source)
XLA Modules:
  0.0 121.3 jit_solution(1317353293528426937)
XLA Ops:
  0.0 119.2 %shard_map.64 = bf16[16,128,128]{2,1,0:T(8,128)(2,1)} custom-call(bf16[4,256,512]{2,1,0:T(8,128)(2,1)} %blocks.1, bf16[8,8,256,128]{3,2,1,0:T(8,128)(2,1)} %bitcast.7, bf16[64,256,128]{2,1,0:T(8,128)(2,1)} %bitcast.8, s32[1,64]{1,0:T(1,128)} %bitcast.9, s32[1,64]{1,0:T(1,128)} %pair_local.1, s32[1,64]{1,0:T(1,128)} %pair_slot.1), custom_call_target="tpu_custom_call" | custom-call | flops 4294967296 | bytes 16777216 | tf_op jit(solution)/shard_map/pallas_call | solution.py:435
  119.2 2.0 %copy.7 = bf16[1,16,128,128]{3,2,1,0:T(8,128)(2,1)} copy(bf16[1,16,128,128]{2,3,1,0:T(8,128)(2,1)} %bitcast.6) | data formatting | bytes 1048576 | tf_op jit(solution)/shard_map/broadcast_in_dim | solution.py:438

commit v4 on v3

--- a/solution.py
+++ b/solution.py
@@ -246,25 +246,24 @@
 
     def first(u):
         k0, k1, m0, m1, _ = UNITS[u]
-        for k in range(k0, k1):
-            for n in range(2 * m0, 2 * m1):
-                half, m = n % 2, n // 2
-                tmp[half] = partial(k, n)
-                stage_a[k, half, m] = tmp[half, part_of(2)].astype(BF16)
-                for d in range(2):
-                    part = tmp[half, part_of(-1 if d else 1)]
-                    if half == d and u not in DIRECT:
-                        acc[k, d, m] = part
-                    else:
-                        stage_b[k, d, half, m] = part.astype(BF16)
-                own[k, half, m] = tmp[half, part_of(0)]
         for half in range(2):
+            for k in range(k0, k1):
+                for m in range(m0, m1):
+                    slot = m % 2
+                    tmp[slot] = partial(k, 2 * m + half)
+                    stage_a[k, half, m] = tmp[slot, part_of(2)].astype(BF16)
+                    for d in range(2):
+                        part = tmp[slot, part_of(-1 if d else 1)]
+                        if half == d and u not in DIRECT:
+                            acc[k, d, m] = part
+                        else:
+                            stage_b[k, d, half, m] = part.astype(BF16)
+                    own[k, half, m] = tmp[slot, part_of(0)]
             device = x_far if u in DIRECT else x_to[half]
             send(a_ref(stage_a, u, half), a_ref(got_a, u, half), a_s.at[u, half], a_r.at[u, half], device)
-        for d in range(2):
-            b_send(u, d, 1 - d)
+            b_send(u, 1 - half, half)
             if u in DIRECT:
-                b_send(u, d, d)
+                b_send(u, half, half)
 
     def second(u):
         if u in DIRECT:

time: 121 us -> 120 us (level)
  no operation moved by 1% of the time
where the time goes in v4:
time: 120 us
  Pallas kernels  118 us (98%)
  local copies, waits for them, and re-layouts  2.04 us (2%)
    pallas_call x1, Pallas kernels, body(): call(blocks, maps, pno_local.reshape(PAIRS, dom, npno), wanted.reshape(1,...  118 us

profile of v4, /device:TPU:1, one launch (start us, length us, event | category | flops | bytes accessed | tf_op | source)
XLA Modules:
  0.0 120.3 jit_solution(9372009988188550183)
XLA Ops:
  0.0 118.2 %shard_map.64 = bf16[16,128,128]{2,1,0:T(8,128)(2,1)} custom-call(bf16[4,256,512]{2,1,0:T(8,128)(2,1)} %blocks.1, bf16[8,8,256,128]{3,2,1,0:T(8,128)(2,1)} %bitcast.7, bf16[64,256,128]{2,1,0:T(8,128)(2,1)} %bitcast.8, s32[1,64]{1,0:T(1,128)} %bitcast.9, s32[1,64]{1,0:T(1,128)} %pair_local.1, s32[1,64]{1,0:T(1,128)} %pair_slot.1), custom_call_target="tpu_custom_call" | custom-call | flops 4294967296 | bytes 16777216 | tf_op jit(solution)/shard_map/pallas_call | solution.py:434
  118.3 2.0 %copy.7 = bf16[1,16,128,128]{3,2,1,0:T(8,128)(2,1)} copy(bf16[1,16,128,128]{2,3,1,0:T(8,128)(2,1)} %bitcast.6) | data formatting | bytes 1048576 | tf_op jit(solution)/shard_map/broadcast_in_dim | solution.py:437
